TPU v7x, 256 devices: a whole 4x4x8 slice. The times are simulated.
256 devices in a mesh: row: 16 (over y, z_lo, core), col: 16 (over x, z_hi).
Axes of the slice: x: 4, y: 4, z: 8 (z_hi: 4, z_lo: 2; z = z_hi * 2 + z_lo), core: 2. Of those that a mesh axis runs over, the one named last changes fastest.
Arguments:
- features: float32 [65536, 256], P(('col', 'row')), may hold values from -6 to 6
- w_self: float32 [256, 256], replicated, may hold values from -0.375 to 0.375
- w_neigh: float32 [256, 256], replicated, may hold values from -0.375 to 0.375
- upstream: float32 [65536, 256], P(('row', 'col')), may hold values from -6 to 6
- tile_coords: int32 [16, 16, 192, 2], P('row', 'col'), may hold values from 0 to 31, as said below
- tile_count: int32 [16, 16], P('row', 'col'), may hold values from 1 to 192, as said below
- tile_bits: int32 [16, 16, 192, 16, 128], P('row', 'col'), may hold values from 0 to 255
Outputs:
- hidden: float32 [65536, 256], P(('row', 'col'))
- grad_features: float32 [65536, 256], P(('col', 'row'))
- grad_self: float32 [256, 256], replicated
- grad_neigh: float32 [256, 256], replicated
Inputs may be any that keep to these rules, and one draw needn't show every extreme that they name: tile_coords[r, c, t, 0] is a block of 128 nodes within the 4096 nodes of row part r, tile_coords[r, c, t, 1] one within the 4096 nodes of column part c; the slots of one device name distinct block pairs; slots at or past tile_count[r, c] carry coordinates and bits that are not part of the adjacency. `tile_count`: some device is full in every draw.
All inputs are finite; a program needn't handle non-finite values.
Results may differ from a plain program's by a relative error of at most 0.0003.
Values sent between devices are 32-bit elements; how exact they have to be, the bound alone decides.
No kernel may reach another device: no remote copies, remote signals or barrier semaphores. Data moves between devices by JAX's collectives and lax.ppermute only.
A program may use at most 128 MiB of HBM per device.

v0:
```python
import math

import jax
import jax.numpy as jnp
from jax import lax
from jax.sharding import PartitionSpec as P

HIGHEST = lax.Precision.HIGHEST


def unpack_tiles(packed):
    shifts = jnp.arange(8, dtype=jnp.int32)
    spread = packed[..., :, None, :] >> shifts[None, :, None] & 1
    spread = spread.reshape(packed.shape[:-2] + (128, 128))
    return jnp.swapaxes(spread, -1, -2).astype(jnp.float32)


def tile_pass(packed, live_mask, coordinates, source, out_blocks, transposed):
    slot_count = packed.shape[0]
    group_size = math.gcd(slot_count, 16)
    feat_width = source.shape[1]
    shaped = source.reshape(source.shape[0] // 128, 128, feat_width)
    picked_ids = coordinates[:, 0] if transposed else coordinates[:, 1]
    target_ids = coordinates[:, 1] if transposed else coordinates[:, 0]
    targets = (target_ids[:, None] == jnp.arange(out_blocks, dtype=jnp.int32)[None, :]).astype(
        jnp.float32
    )

    def advance(state_pair, pieces):
        running, counts = state_pair
        bits_group, live_group, picked_group, target_group = pieces
        squares = unpack_tiles(bits_group) * live_group[:, None, None]
        blocks = shaped[picked_group]
        if transposed:
            product = jnp.einsum("tij,tif->tjf", squares, blocks, precision=HIGHEST)
        else:
            product = jnp.einsum("tij,tjf->tif", squares, blocks, precision=HIGHEST)
            counts = counts + jnp.einsum(
                "tb,ti->bi", target_group, jnp.sum(squares, axis=2), precision=HIGHEST
            )
        running = running + jnp.einsum("tb,tif->bif", target_group, product, precision=HIGHEST)
        return ((running, counts), None)

    turns = slot_count // group_size
    pieces = (
        packed.reshape(turns, group_size, 16, 128),
        live_mask.reshape(turns, group_size),
        picked_ids.reshape(turns, group_size),
        targets.reshape(turns, group_size, out_blocks),
    )
    start = (
        jnp.zeros((out_blocks, 128, feat_width), jnp.float32),
        jnp.zeros((out_blocks, 128), jnp.float32),
    )
    (running, counts), _ = lax.scan(advance, start, pieces)
    return (running.reshape(out_blocks * 128, feat_width), counts.reshape(out_blocks * 128))


def gate_grad(cotangent, preact):
    gate_sigmoid = jax.nn.sigmoid(preact)
    return cotangent * gate_sigmoid * (1.0 + preact * (1.0 - gate_sigmoid))


def local(features, w_self, w_neigh, upstream, tile_coords, tile_count, tile_bits):
    row_devices = lax.axis_size("row")
    col_devices = lax.axis_size("col")
    row_index = lax.axis_index("row")
    col_index = lax.axis_index("col")
    rows_dev, feat_width = features.shape
    row_part = rows_dev * col_devices
    column_part = rows_dev * row_devices
    row_blocks = row_part // 128
    column_blocks = column_part // 128
    coordinates = tile_coords[0, 0]
    packed = tile_bits[0, 0]
    slot_count = coordinates.shape[0]
    live_mask = (jnp.arange(slot_count, dtype=jnp.int32) < tile_count[0, 0]).astype(jnp.float32)
    part_ratio = col_devices // row_devices
    inside = col_index // part_ratio == row_index
    gathered = lax.all_gather(features, "row", axis=0, tiled=True)
    partial_sum, local_degree = tile_pass(
        packed, live_mask, coordinates, gathered, row_blocks, False
    )
    degree = lax.psum(local_degree, "col")
    inverse = 1.0 / jnp.maximum(degree, 1.0)
    partial_value = jnp.dot(partial_sum * inverse[:, None], w_neigh, precision=HIGHEST)

    def add_self(running):
        own_term = jnp.dot(gathered, w_self, precision=HIGHEST)
        return running + own_term

    partial_value = lax.cond(inside, add_self, lambda running: running, partial_value)
    preactivation = lax.psum_scatter(partial_value, "col", scatter_dimension=0, tiled=True)
    hidden = preactivation * jax.nn.sigmoid(preactivation)
    grad_pre = gate_grad(upstream, preactivation)
    grad_rows = lax.all_gather(grad_pre, "col", axis=0, tiled=True)
    scaled = grad_rows * inverse[:, None]
    back_sum, _ = tile_pass(packed, live_mask, coordinates, scaled, column_blocks, True)
    back_proj = jnp.dot(back_sum, w_neigh.T, precision=HIGHEST)

    def add_self_back(running):
        return running + jnp.dot(grad_rows, w_self.T, precision=HIGHEST)

    back_proj = lax.cond(inside, add_self_back, lambda running: running, back_proj)

    def self_product(operand):
        return jnp.einsum("nf,ng->fg", gathered, grad_rows, precision=HIGHEST)

    def no_product(operand):
        return jnp.zeros((feat_width, feat_width), jnp.float32)

    grad_self_part = lax.cond(inside, self_product, no_product, 0)
    grad_features = lax.psum_scatter(back_proj, "row", scatter_dimension=0, tiled=True)
    grad_neigh_part = jnp.einsum("nf,ng->fg", partial_sum, scaled, precision=HIGHEST)
    grad_self, grad_neigh = lax.psum((grad_self_part, grad_neigh_part), ("row", "col"))
    return (hidden, grad_features, grad_self, grad_neigh)


def solution(mesh):
    return jax.shard_map(
        local,
        mesh=mesh,
        in_specs=(
            P(("col", "row"), None),
            P(),
            P(),
            P(("row", "col"), None),
            P("row", "col", None, None),
            P("row", "col"),
            P("row", "col", None, None, None),
        ),
        out_specs=(P(("row", "col"), None), P(("col", "row"), None), P(), P()),
        check_vma=False,
    )
```

profile of v0, /device:TPU:38, one launch (start us, length us, event | category | flops | bytes accessed | tf_op | source)
XLA Modules:
  0.0 1068.8 jit_solution(404264227895118599)
XLA Ops:
  9.7 42.6 %all-gather.3.cloned.1.call-done = f32[4096,256]{1,0:T(8,128)} async-done(((f32[256,256]{1,0:T(8,128)}), f32[4096,256]{1,0:T(8,128)}) %all-gather.3.cloned.1.call-update) | async-done | bytes 4194320 | tf_op jit(solution)/shard_map/all_gather | solution.py:80
  52.3 191.6 %while.24 = (s32[]{:T(128)}, f32[32,128,256]{2,0,1:T(8,128)}, f32[32,128]{1,0:T(8,128)S(1)}, f32[12,16,32]{2,1,0:T(8,128)S(1)}, s32[12,16,16,128]{3,2,1,0:T(8,12...) while((s32[]{:T(128)}, f32[32,128,256]{2,0,1:T(8,128)}, ...), condition=%wide.region_2.3_spmd.clone, body=%wide.region_0.2_spmd.clone.sunk | while | flops 1011883072 | bytes 19471492 | solution.py:55
  75.0 8.1 select_add_fusion.4
  91.0 8.1 select_add_fusion.4
  107.0 8.1 select_add_fusion.4
  123.0 8.1 select_add_fusion.4
  139.1 8.1 select_add_fusion.4
  155.1 8.1 select_add_fusion.4
  171.1 8.1 select_add_fusion.4
  187.1 8.1 select_add_fusion.4
  203.2 8.1 select_add_fusion.4
  219.2 8.1 select_add_fusion.4
  235.2 8.1 select_add_fusion.4
  250.4 75.3 %psum.21 = f32[4096]{0:T(1024)S(1)} all-reduce(f32[4096]{0:T(1024)S(1)} %bitcast.119), channel_id=1, replica_groups=mesh['row'=16,'col'=16] {'col'}, use_global_device_ids=true, to_apply=%region_3.4 | all-reduce | flops 4096 | bytes 32768 | tf_op jit(solution)/shard_map/psum | solution.py:84
  333.4 10.7 %conditional.3 = (f32[4096,256]{1,0:T(8,128)}) conditional(s32[]{:T(128)} %convert_element_type.25, f32[4096,256]{1,0:T(8,128)} %fusion.38, (f32[4096,256]{1,0:T(8,128)}, f32[256,256]{1,0:T(8,128)S(1)}, f32[4096,256]{1,0:T(8,128)}) %tuple.97), branch_computations={%region_4.5_spmd, %region_5.6_spmd} | conditional | flops 3222274048 | bytes 12845064 | solution.py:92
  344.2 101.7 %reduce-scatter.3.cloned.1.call-done = f32[256,256]{1,0:T(8,128)} async-done(((f32[4096,256]{1,0:T(8,128)}), f32[256,256]{1,0:T(8,128)}) %reduce-scatter.3.cloned.1.call-update) | async-done | bytes 262160 | tf_op jit(solution)/shard_map/reduce_scatter | solution.py:93
  448.0 77.9 %all-gather.5.cloned.1.call-done = f32[4096,256]{1,0:T(8,128)} async-done(((f32[256,256]{1,0:T(8,128)}), f32[4096,256]{1,0:T(8,128)}) %all-gather.5.cloned.1.call-update) | async-done | bytes 4194320 | tf_op jit(solution)/shard_map/all_gather | solution.py:96
  536.8 184.5 %while.25 = (s32[]{:T(128)}, f32[32,128,256]{2,0,1:T(8,128)}, f32[12,16,32]{2,1,0:T(8,128)S(1)}, s32[12,16,16,128]{3,2,1,0:T(8,128)}, f32[12,16]{1,0:T(8,128)S(1...) while((s32[]{:T(128)}, f32[32,128,256]{2,0,1:T(8,128)}, ...), condition=%wide.region_8.9_spmd.clone, body=%wide.region_7.8_spmd.clone.sunk | while | flops 1009779776 | bytes 19282488 | solution.py:55
  574.3 8.1 select_add_fusion.5
  589.8 8.1 select_add_fusion.5
  682.4 8.1 select_add_fusion.5
  713.2 8.1 select_add_fusion.5
  736.3 250.5 %all-reduce.3.cloned.1.call-done = (f32[256,256]{1,0:T(8,128)}, f32[256,256]{1,0:T(8,128)}) async-done(((f32[256,256]{1,0:T(8,128)}, f32[256,256]{1,0:T(8,128)}), (f32[256,256]{1,0:T(8,128)}, f32[256,256]{1,0:T(8,128)})) %all-reduce.3.cloned.1.call-update) | async-done | bytes 524304 | tf_op jit(solution)/shard_map/psum | solution.py:115
  986.8 71.8 %reduce-scatter.5.cloned.1.call-done = f32[256,256]{1,0:T(8,128)} async-done(((f32[4096,256]{1,0:T(8,128)}), f32[256,256]{1,0:T(8,128)}) %reduce-scatter.5.cloned.1.call-update) | async-done | bytes 262160 | tf_op jit(solution)/shard_map/reduce_scatter | solution.py:113
  (269 shorter events, 300.1 us)
Async XLA Ops:
  7.2 318.6 %copy-start = (f32[256,256]{1,0:T(8,128)S(1)}, f32[256,256]{1,0:T(8,128)}, u32[]{:S(2)}) copy-start(f32[256,256]{1,0:T(8,128)} %param.19) | copy-start | bytes 786436
  7.2 45.1 %all-gather.3.cloned.1.call-start = ((), (), s32[]{:S(2)}) async-start(), calls=%async_computation.2 | async-start | bytes 4456448 | tf_op jit(solution)/shard_map/all_gather | solution.py:80
  7.9 438.1 %reduce-scatter.3.cloned.1.call-start = ((), (), s32[]{:S(2)}) async-start(), calls=%async_computation.3 | async-start | bytes 4456448 | tf_op jit(solution)/shard_map/reduce_scatter | solution.py:93
  325.8 7.7 copy-start.3
  344.2 101.8 %copy-start.5 = (f32[256,256]{1,0:T(8,128)S(1)}, f32[256,256]{1,0:T(8,128)}, u32[]{:S(2)}) copy-start(f32[256,256]{1,0:T(8,128)} %param.20) | copy-start | bytes 786436
  344.2 181.7 %all-gather.5.cloned.1.call-start = ((), (), s32[]{:S(2)}) async-start(), calls=%async_computation.4 | async-start | bytes 4456448 | tf_op jit(solution)/shard_map/all_gather | solution.py:96
  447.8 538.9 %all-reduce.3.cloned.1.call-start = ((), (), s32[]{:S(2)}) async-start(), calls=%async_computation.6 | async-start | bytes 1048576 | tf_op jit(solution)/shard_map/psum | solution.py:115
  525.9 3.4 copy-start.2
  529.4 7.5 copy-start.1
  727.9 0.7 copy-start.4
  728.7 329.9 %reduce-scatter.5.cloned.1.call-start = ((), (), s32[]{:S(2)}) async-start(), calls=%async_computation.5 | async-start | bytes 4456448 | tf_op jit(solution)/shard_map/reduce_scatter | solution.py:113
Sparse Core Ops, SparseCore 0:
  9.9 42.3 all-gather.2
  344.3 101.6 reduce-scatter.2
  449.3 76.5 all-gather.4
  728.8 257.9 all-reduce.2
  989.9 68.5 reduce-scatter.4
where the time goes:
time: 1080 us; the launch traced here: 1070 us
  waiting for transfers between devices  545 us (50%)
  matrix products  301 us (28%)
  local copies, waits for them, and re-layouts  112 us (10%)
  blocking collectives  75.3 us (7%)
  between operations  15 us (1%)
  loops' own time  12 us (1%)
    psum x1, waiting for transfers between devices, local(): lax.psum((grad_self_part, grad_neigh_part), ('row', 'col'))  250 us
    dot_general x24, matrix products, advance(): jnp.einsum('tb,tif->bif', target_group, product, precision=HIGHEST)  194 us
    reduce_scatter x1, waiting for transfers between devices, local(): lax.psum_scatter(partial_value, 'col', scatter_dimension=0, tiled=True)  102 us
    all_gather x1, waiting for transfers between devices, local(): grad_rows = lax.all_gather(grad_pre, 'col', axis=0, tiled=True)  77.9 us
    psum x1, blocking collectives, local(): degree = lax.psum(local_degree, 'col')  75.3 us
    reduce_scatter x1, waiting for transfers between devices, local(): lax.psum_scatter(back_proj, 'row', scatter_dimension=0, tiled=True)  71.8 us
    gather x24, local copies, waits for them, and re-layouts, advance(): blocks = shaped[picked_group]  68.9 us
    all_gather x1, waiting for transfers between devices, local(): gathered = lax.all_gather(features, 'row', axis=0, tiled=True)  42.6 us
  transfers between devices with their start and end apart: 5, of which 5 were waited for; matrix products, arithmetic and copies ran while one was open for 1% of the time, Pallas kernels for 0%

commit v1 on v0

v1 whole, which is shorter than its diff:
```python
import functools

import jax
import jax.numpy as jnp
from jax import lax
from jax.experimental import pallas as pl
from jax.experimental.pallas import tpu as pltpu
from jax.sharding import PartitionSpec as P

HIGH = lax.Precision.HIGH
UNROLL = 8
BLOCK = 128
DEGREE_ROWS = 8

SMEM = pl.BlockSpec(memory_space=pltpu.SMEM)
VMEM = pl.BlockSpec(memory_space=pltpu.VMEM)


def split_halves(value):
    high = value.astype(jnp.bfloat16)
    low = (value - high.astype(jnp.float32)).astype(jnp.bfloat16)
    return high, low


def unpack(words):
    shift = lax.broadcasted_iota(jnp.int32, (16, 8, BLOCK), 1)
    spread = jnp.broadcast_to(words[:, None, :], (16, 8, BLOCK))
    return ((spread >> shift) & 1).reshape(BLOCK, BLOCK).astype(jnp.float32)


def tile_loop(count_ref, coords_ref, bits_ref, visit):
    count = count_ref[0, 0]

    def step(group, carry):
        for offset in range(UNROLL):
            slot = group * UNROLL + offset
            mask = jnp.where(slot < count, 255, 0)
            tile = unpack(bits_ref[slot] & mask)
            visit(coords_ref[slot, 0], coords_ref[slot, 1], tile)
        return carry

    lax.fori_loop(0, (count + UNROLL - 1) // UNROLL, step, 0)


def forward_kernel(count_ref, coords_ref, bits_ref, x_ref, out_ref, pieces):
    feat = x_ref.shape[1]

    def prepare(shard, carry):
        for half in range(2):
            high, low = split_halves(x_ref[shard, :, half * BLOCK : (half + 1) * BLOCK])
            pieces[2 * shard + half, :, 0:BLOCK] = high
            pieces[2 * shard + half, :, BLOCK : 2 * BLOCK] = low
        return carry

    lax.fori_loop(0, x_ref.shape[0], prepare, 0)
    out_ref[...] = jnp.zeros_like(out_ref)

    def visit(i, j, tile):
        narrow = tile.astype(jnp.bfloat16)
        out_ref[i, 0:feat, :] += jnp.dot(
            pieces[j],
            jnp.concatenate([narrow, narrow], axis=0),
            preferred_element_type=jnp.float32,
        )
        out_ref[i, feat : feat + DEGREE_ROWS, :] += tile.reshape(16, 8, BLOCK).sum(0)

    tile_loop(count_ref, coords_ref, bits_ref, visit)


def backward_kernel(count_ref, coords_ref, bits_ref, g_ref, out_ref, pieces):
    def prepare(block, carry):
        high, low = split_halves(g_ref[block])
        pieces[block, 0:BLOCK, :] = high
        pieces[block, BLOCK : 2 * BLOCK, :] = low
        return carry

    lax.fori_loop(0, g_ref.shape[0], prepare, 0)
    out_ref[...] = jnp.zeros_like(out_ref)

    def visit(i, j, tile):
        narrow = tile.astype(jnp.bfloat16)
        out_ref[j] += jnp.dot(
            jnp.concatenate([narrow, narrow], axis=1),
            pieces[i],
            preferred_element_type=jnp.float32,
        )

    tile_loop(count_ref, coords_ref, bits_ref, visit)


def run_tiles(kernel, count, coords, bits, source, out_shape, name):
    feat_blocks = source.size // (BLOCK * 256)
    work = 2 * 2 * bits.shape[0] * BLOCK * BLOCK * 256
    return pl.pallas_call(
        kernel,
        out_shape=jax.ShapeDtypeStruct(out_shape, jnp.float32),
        in_specs=[SMEM, SMEM, VMEM, VMEM],
        out_specs=VMEM,
        scratch_shapes=[pltpu.VMEM((feat_blocks, 256, 256), jnp.bfloat16)],
        compiler_params=pltpu.CompilerParams(vmem_limit_bytes=40 * 2**20),
        cost_estimate=pl.CostEstimate(
            flops=work, bytes_accessed=10 * 2**20, transcendentals=0
        ),
        name=name,
    )(count, coords, bits, source)


def exchange(value, axis, size, stride):
    devices = lax.axis_size(axis)

    def partner(index, distance):
        digit = index // stride % size
        return index + ((digit + distance) % size - digit) * stride

    def send(piece, distance):
        pairs = [(index, partner(index, distance)) for index in range(devices)]
        return lax.ppermute(piece, axis, pairs)

    return lax.axis_index(axis) // stride % size, send


GROUPS = (("row", 2, 1), ("row", 2, 2), ("row", 4, 4), ("col", 4, 1), ("col", 4, 4))


def sum_everywhere(value):
    for axis, size, stride in GROUPS:
        digit, send = exchange(value, axis, size, stride)
        rows = value.shape[0] // size

        def part(which, value=value, rows=rows):
            return lax.dynamic_slice_in_dim(value, which * rows, rows, 0)

        total = part(digit)
        for distance in range(1, size):
            total = total + send(part((digit + distance) % size), distance)
        value = total
    for axis, size, stride in reversed(GROUPS):
        digit, send = exchange(value, axis, size, stride)
        rows = value.shape[0]
        whole = jnp.zeros((rows * size,) + value.shape[1:], value.dtype)
        whole = lax.dynamic_update_slice_in_dim(whole, value, digit * rows, 0)
        for distance in range(1, size):
            origin = (digit + size - distance) % size
            whole = lax.dynamic_update_slice_in_dim(
                whole, send(value, distance), origin * rows, 0
            )
        value = whole
    return value


def local(features, w_self, w_neigh, upstream, tile_coords, tile_count, tile_bits):
    devices = lax.axis_size("row")
    rows_dev, feat = features.shape
    blocks = rows_dev * devices // BLOCK
    coords, bits = tile_coords[0, 0], tile_bits[0, 0]
    swap = [
        (r * devices + c, c * devices + r) for r in range(devices) for c in range(devices)
    ]

    gathered = lax.all_gather(features.T, "row", axis=0, tiled=False)
    own = lax.ppermute(features, ("row", "col"), swap)
    sums = run_tiles(
        forward_kernel,
        tile_count,
        coords,
        bits,
        gathered,
        (blocks, feat + DEGREE_ROWS, BLOCK),
        "forward",
    )
    sums = lax.psum_scatter(sums, "col", scatter_dimension=0, tiled=True)
    degree = sums[:, feat:, :].sum(1)
    inverse = 1.0 / jnp.maximum(degree, 1.0)
    aggregate = (sums[:, :feat, :] * inverse[:, None, :]).swapaxes(1, 2)
    aggregate = aggregate.reshape(rows_dev, feat)
    inverse = inverse.reshape(rows_dev, 1)
    preact = jnp.dot(own, w_self, precision=HIGH) + jnp.dot(
        aggregate, w_neigh, precision=HIGH
    )
    gate = jax.nn.sigmoid(preact)
    hidden = preact * gate
    grad_pre = upstream * gate * (1.0 + preact * (1.0 - gate))

    grad_rows = lax.all_gather(grad_pre * inverse, "col", axis=0, tiled=True)
    grad_own = lax.ppermute(grad_pre, ("row", "col"), swap)
    weights = jnp.dot(
        jnp.concatenate([own, aggregate], axis=1).T, grad_pre, precision=HIGH
    )
    weights = sum_everywhere(weights)
    back = run_tiles(
        backward_kernel,
        tile_count,
        coords,
        bits,
        grad_rows.reshape(blocks, BLOCK, feat),
        (blocks, BLOCK, feat),
        "backward",
    )
    back = lax.psum_scatter(
        back.reshape(blocks * BLOCK, feat), "row", scatter_dimension=0, tiled=True
    )
    grad_features = jnp.dot(grad_own, w_self.T, precision=HIGH) + jnp.dot(
        back, w_neigh.T, precision=HIGH
    )
    return hidden, grad_features, weights[:feat], weights[feat:]


def solution(mesh):
    return jax.shard_map(
        local,
        mesh=mesh,
        in_specs=(
            P(("col", "row"), None),
            P(),
            P(),
            P(("row", "col"), None),
            P("row", "col", None, None),
            P("row", "col"),
            P("row", "col", None, None, None),
        ),
        out_specs=(P(("row", "col"), None), P(("col", "row"), None), P(), P()),
        check_vma=False,
    )
```

time: 1080 us -> 366 us (0.34); the launches traced: 1070 us -> 368 us
  matrix products: 301 us -> 4.36 us
  waiting for transfers between devices: 545 us -> 270 us
  local copies, waits for them, and re-layouts: 112 us -> 17 us
  blocking collectives: 75.3 us -> 0 us
  starting transfers between devices: 0.2 us -> 36.5 us
  Pallas kernels: 0 us -> 22.9 us
  loops' own time: 12 us -> 0 us
    dot_general x63 -> x5, matrix products: 301 us -> 4.36 us  [the longest x1 1.29 us: local(): jnp.dot(back, w_neigh.T, precision=HIGH)]
    psum x1 -> x0, waiting for transfers between devices: 250 us -> none  [local(): lax.psum((grad_self_part, grad_neigh_part), ('row', 'col'))]
    reduce_scatter x2, waiting for transfers between devices: 173 us -> 97.9 us  [the longest x1 97.9 us: local(): sums = lax.psum_scatter(sums, 'col', scatter_dimension=0, tiled=True)]
    psum x1 -> x0, blocking collectives: 75.3 us -> none  [local(): degree = lax.psum(local_degree, 'col')]
    gather x24 -> x0, local copies, waits for them, and re-layouts: 68.9 us -> none  [advance(): blocks = shaped[picked_group]]
    ppermute x0 -> x24, waiting for transfers between devices: none -> 52.2 us  [the longest x22 36.6 us: send(): return lax.ppermute(piece, axis, pairs)]
    ppermute x0 -> x24, starting transfers between devices: none -> 36.3 us  [the longest x22 28.6 us: send(): return lax.ppermute(piece, axis, pairs)]
    shift_right_arithmetic x72 -> x0, local copies, waits for them, and re-layouts: 24.2 us -> none  [unpack_tiles(): spread = packed[..., :, None, :] >> shifts[None, :, None] & 1]
  transfers between devices with their start and end apart: 5 -> 28, of which waited for: 5 -> 21; matrix products, arithmetic and copies ran while one was open for 1% -> 2% of each run, Pallas kernels for 0% -> 0%
where the time goes in v1:
time: 366 us; the launch traced here: 368 us
  waiting for transfers between devices  270 us (74%)
  starting transfers between devices  36.5 us (10%)
  Pallas kernels  22.9 us (6%)
  local copies, waits for them, and re-layouts  17 us (5%)
  between operations  14.9 us (4%)
  matrix products  4.36 us (1%)
    reduce_scatter x1, waiting for transfers between devices, local(): sums = lax.psum_scatter(sums, 'col', scatter_dimension=0, tiled=True)  97.9 us
    all_gather x1, waiting for transfers between devices, local(): grad_rows = lax.all_gather(grad_pre * inverse, 'col', axis=0, tiled=True)  76.7 us
    all_gather x1, waiting for transfers between devices, local(): gathered = lax.all_gather(features.T, 'row', axis=0, tiled=False)  42.8 us
    ppermute x22, waiting for transfers between devices, send(): return lax.ppermute(piece, axis, pairs)  36.6 us
    ppermute x22, starting transfers between devices, send(): return lax.ppermute(piece, axis, pairs)  28.6 us
    pallas_call x2, Pallas kernels, run_tiles(): pl.pallas_call(kernel, out_shape=jax.ShapeDtypeStruct(out_shape, jnp.floa...  22.9 us
    ppermute x1, waiting for transfers between devices, local(): grad_own = lax.ppermute(grad_pre, ('row', 'col'), swap)  15.6 us
    unnamed x19, local copies, waits for them, and re-layouts  10 us
  transfers between devices with their start and end apart: 28, of which 21 were waited for; matrix products, arithmetic and copies ran while one was open for 2% of the time, Pallas kernels for 0%

profile of v1, /device:TPU:38, one launch (start us, length us, event | category | flops | bytes accessed | tf_op | source)
XLA Modules:
  0.0 367.8 jit_solution(1016857549750071479)
XLA Ops:
  9.4 42.8 %all-gather.6.cloned.1.call-done = f32[4096,256]{0,1:T(8,128)} async-done(((f32[256,256]{0,1:T(8,128)}), f32[4096,256]{0,1:T(8,128)}) %all-gather.6.cloned.1.call-update) | async-done | bytes 4194320 | tf_op jit(solution)/shard_map/all_gather | solution.py:160
  52.2 5.7 %copy.14 = f32[4096,256]{1,0:T(8,128)} copy(f32[4096,256]{0,1:T(8,128)} %all-gather.6.cloned.1.call-done) | data formatting | bytes 8388608 | tf_op jit(solution)/shard_map/all_gather | solution.py:160
  57.9 2.2 copy-done.3
  60.1 13.0 %forward.1 = f32[32,264,128]{2,1,0:T(8,128)S(1)} custom-call(s32[1,1]{1,0:T(1,128)S(6)} %copy.32.count_ref, s32[192,2]{1,0:T(8,128)S(1)} %bitcast.22, s32[192,16,128]{2,1,0:T(8,128)S(1)} %bitcast.25, f32[16,256,256]{2,1,0:T(8,128)S(1)} %bitcast.21), custom_call_target="tpu_custom_call" | custom-call | flops 3221225472 | bytes 10485760 | tf_op jit(solution)/shard_map/forward/pallas_call | solution.py:94
  73.1 2.0 copy-done.1
  76.0 2.2 collective-permute-start
  78.3 97.9 %reduce-scatter.3.cloned.1.call-done = f32[2,264,128]{2,1,0:T(8,128)} async-done(((f32[32,264,128]{2,1,0:T(8,128)}), f32[2,264,128]{2,1,0:T(8,128)}) %reduce-scatter.3.cloned.1.call-update) | async-done | bytes 270352 | tf_op jit(solution)/shard_map/reduce_scatter | solution.py:171
  179.6 76.7 %all-gather.4.cloned.1.call-done = f32[4096,256]{1,0:T(8,128)} async-done(((f32[256,256]{1,0:T(8,128)}), f32[4096,256]{1,0:T(8,128)}) %all-gather.4.cloned.1.call-update) | async-done | bytes 4194320 | tf_op jit(solution)/shard_map/all_gather | solution.py:184
  256.3 2.2 copy-done.4
  258.5 9.9 %backward.1 = f32[32,128,256]{2,1,0:T(8,128)S(1)} custom-call(s32[1,1]{1,0:T(1,128)S(6)} %copy.32.count_ref, s32[192,2]{1,0:T(8,128)S(1)} %bitcast.23, s32[192,16,128]{2,1,0:T(8,128)S(1)} %bitcast.26, f32[32,128,256]{2,1,0:T(8,128)S(1)} %bitcast.24), custom_call_target="tpu_custom_call" | custom-call | flops 3221225472 | bytes 10485760 | tf_op jit(solution)/shard_map/backward/pallas_call | solution.py:94
  273.0 5.4 %collective-permute-done.3 = f32[128,256]{1,0:T(8,128)S(1)} collective-permute-done((f32[128,256]{1,0:T(8,128)S(1)}, f32[128,256]{1,0:T(8,128)S(1)}, u32[]{:S(2)}, u32[]{:S(2)}) %collective-permute-start.3) | collective-permute-done | bytes 131104 | tf_op jit(solution)/shard_map/ppermute | solution.py:117
  278.5 2.0 collective-permute-start.4
  280.5 2.4 collective-permute-start.5
  288.1 2.5 collective-permute-start.8
  293.1 2.8 collective-permute-done.8
  296.5 2.8 collective-permute-start.11
  299.6 2.0 collective-permute-done.11
  301.6 2.5 collective-permute-done.12
  310.6 3.2 collective-permute-start.16
  317.6 3.8 %collective-permute-done.17 = f32[8,256]{1,0:T(8,128)S(1)} collective-permute-done((f32[8,256]{1,0:T(8,128)S(1)}, f32[8,256]{1,0:T(8,128)S(1)}, u32[]{:S(2)}, u32[]{:S(2)}) %collective-permute-start.17) | collective-permute-done | bytes 8224 | tf_op jit(solution)/shard_map/ppermute | solution.py:117
  321.9 3.6 collective-permute-start.20
  330.1 6.6 %collective-permute-done.22 = f32[128,256]{1,0:T(8,128)S(1)} collective-permute-done((f32[128,256]{1,0:T(8,128)S(1)}, f32[128,256]{1,0:T(8,128)S(1)}, u32[]{:S(2)}, u32[]{:S(2)}) %collective-permute-start.22) | collective-permute-done | bytes 131104 | tf_op jit(solution)/shard_map/ppermute | solution.py:117
  336.8 5.5 %collective-permute-start.1 = (f32[256,256]{1,0:T(8,128)S(1)}, f32[256,256]{1,0:T(8,128)S(1)}, u32[]{:S(2)}, u32[]{:S(2)}) collective-permute-start(f32[256,256]{1,0:T(8,128)S(1)} %get-tuple-element.7), channel_id=1, source_target_pairs={{0,0},{1,16},{2,32},{3,48},{4,64},{5,80},{6,96},{7,112},{8,128},{9... | collective-permute-start | bytes 786440 | tf_op jit(solution)/shard_map/ppermute | solution.py:185
  344.6 15.6 %collective-permute-done.1 = f32[256,256]{1,0:T(8,128)S(1)} collective-permute-done((f32[256,256]{1,0:T(8,128)S(1)}, f32[256,256]{1,0:T(8,128)S(1)}, u32[]{:S(2)}, u32[]{:S(2)}) %collective-permute-start.1) | collective-permute-done | bytes 262176 | tf_op jit(solution)/shard_map/ppermute | solution.py:185
  (99 shorter events, 37.5 us)
Async XLA Ops:
  7.2 45.0 %all-gather.6.cloned.1.call-start = ((), (), s32[]{:S(2)}) async-start(), calls=%async_computation.5 | async-start | bytes 4456448 | tf_op jit(solution)/shard_map/all_gather | solution.py:160
  7.9 168.3 %reduce-scatter.3.cloned.1.call-start = ((), (), s32[]{:S(2)}) async-start(), calls=%async_computation.2 | async-start | bytes 4595712 | tf_op jit(solution)/shard_map/reduce_scatter | solution.py:171
  75.1 181.2 %all-gather.4.cloned.1.call-start = ((), (), s32[]{:S(2)}) async-start(), calls=%async_computation.3 | async-start | bytes 4456448 | tf_op jit(solution)/shard_map/all_gather | solution.py:184
  76.0 102.3 %collective-permute-start = (f32[256,256]{1,0:T(8,128)S(1)}, f32[256,256]{1,0:T(8,128)S(1)}, u32[]{:S(2)}, u32[]{:S(2)}) collective-permute-start(f32[256,256]{1,0:T(8,128)S(1)} %copy-done.8), channel_id=1, source_target_pairs={{0,0},{1,16},{2,32},{3,48},{4,64},{5,80},{6,96},{7,112},{8,128},{9... | collective-permute-start | bytes 786440 | tf_op jit(solution)/shard_map/ppermute | solution.py:161
  179.5 163.8 %reduce-scatter.5.cloned.1.call-start = ((), (), s32[]{:S(2)}) async-start(), calls=%async_computation.4 | async-start | bytes 4456448 | tf_op jit(solution)/shard_map/reduce_scatter | solution.py:199
  272.8 5.6 %collective-permute-start.3 = (f32[128,256]{1,0:T(8,128)S(1)}, f32[128,256]{1,0:T(8,128)S(1)}, u32[]{:S(2)}, u32[]{:S(2)}) collective-permute-start(f32[128,256]{1,0:T(8,128)S(1)} %constant_dynamic-slice_fusion.10), channel_id=1, source_target_pairs={{0,32},{16,48},{32,0},{48,16},{64,96},{80,112},{96,64},{112,80},{1... | collective-permute-start | bytes 393224 | tf_op jit(solution)/shard_map/ppermute | solution.py:117
  278.5 5.7 %collective-permute-start.4 = (f32[32,256]{1,0:T(8,128)S(1)}, f32[32,256]{1,0:T(8,128)S(1)}, u32[]{:S(2)}, u32[]{:S(2)}) collective-permute-start(f32[32,256]{1,0:T(8,128)S(1)} %get-tuple-element.11), channel_id=1, source_target_pairs={{0,64},{16,80},{32,96},{48,112},{64,128},{80,144},{96,160},{112,17... | collective-permute-start | bytes 98312 | tf_op jit(solution)/shard_map/ppermute | solution.py:117
  280.5 5.4 %collective-permute-start.5 = (f32[32,256]{1,0:T(8,128)S(1)}, f32[32,256]{1,0:T(8,128)S(1)}, u32[]{:S(2)}, u32[]{:S(2)}) collective-permute-start(f32[32,256]{1,0:T(8,128)S(1)} %get-tuple-element.13), channel_id=1, source_target_pairs={{0,128},{16,144},{32,160},{48,176},{64,192},{80,208},{96,224},{112... | collective-permute-start | bytes 98312 | tf_op jit(solution)/shard_map/ppermute | solution.py:117
  282.9 4.2 %collective-permute-start.6 = (f32[32,256]{1,0:T(8,128)S(1)}, f32[32,256]{1,0:T(8,128)S(1)}, u32[]{:S(2)}, u32[]{:S(2)}) collective-permute-start(f32[32,256]{1,0:T(8,128)S(1)} %get-tuple-element.12), channel_id=1, source_target_pairs={{0,192},{16,208},{32,224},{48,240},{64,0},{80,16},{96,32},{112,48}... | collective-permute-start | bytes 98312 | tf_op jit(solution)/shard_map/ppermute | solution.py:117
  287.2 5.9 %collective-permute-start.7 = (f32[8,256]{1,0:T(8,128)S(1)}, f32[8,256]{1,0:T(8,128)S(1)}, u32[]{:S(2)}, u32[]{:S(2)}) collective-permute-start(f32[8,256]{1,0:T(8,128)S(1)} %get-tuple-element.14), channel_id=1, source_target_pairs={{0,1},{1,2},{2,3},{3,0},{4,5},{5,6},{6,7},{7,4},{8,9},{9,10},{10,1... | collective-permute-start | bytes 24584 | tf_op jit(solution)/shard_map/ppermute | solution.py:117
  288.1 7.8 %collective-permute-start.8 = (f32[8,256]{1,0:T(8,128)S(1)}, f32[8,256]{1,0:T(8,128)S(1)}, u32[]{:S(2)}, u32[]{:S(2)}) collective-permute-start(f32[8,256]{1,0:T(8,128)S(1)} %get-tuple-element.16), channel_id=1, source_target_pairs={{0,2},{1,3},{2,0},{3,1},{4,6},{5,7},{6,4},{7,5},{8,10},{9,11},{10,... | collective-permute-start | bytes 24584 | tf_op jit(solution)/shard_map/ppermute | solution.py:117
  290.6 5.3 %collective-permute-start.9 = (f32[8,256]{1,0:T(8,128)S(1)}, f32[8,256]{1,0:T(8,128)S(1)}, u32[]{:S(2)}, u32[]{:S(2)}) collective-permute-start(f32[8,256]{1,0:T(8,128)S(1)} %get-tuple-element.15), channel_id=1, source_target_pairs={{0,3},{1,0},{2,1},{3,2},{4,7},{5,4},{6,5},{7,6},{8,11},{9,8},{10,9... | collective-permute-start | bytes 24584 | tf_op jit(solution)/shard_map/ppermute | solution.py:117
  296.5 5.1 %collective-permute-start.11 = (f32[2,256]{1,0:T(2,128)S(1)}, f32[2,256]{1,0:T(2,128)S(1)}, u32[]{:S(2)}, u32[]{:S(2)}) collective-permute-start(f32[2,256]{1,0:T(2,128)S(1)} %get-tuple-element.19), channel_id=1, source_target_pairs={{0,8},{1,9},{2,10},{3,11},{4,12},{5,13},{6,14},{7,15},{8,0},{9,1},... | collective-permute-start | bytes 6152 | tf_op jit(solution)/shard_map/ppermute | solution.py:117
  299.3 4.8 %collective-permute-start.12 = (f32[2,256]{1,0:T(2,128)S(1)}, f32[2,256]{1,0:T(2,128)S(1)}, u32[]{:S(2)}, u32[]{:S(2)}) collective-permute-start(f32[2,256]{1,0:T(2,128)S(1)} %get-tuple-element.18), channel_id=1, source_target_pairs={{0,12},{1,13},{2,14},{3,15},{4,0},{5,1},{6,2},{7,3},{8,4},{9,5},{1... | collective-permute-start | bytes 6152 | tf_op jit(solution)/shard_map/ppermute | solution.py:117
  304.6 5.1 %collective-permute-start.14 = (f32[2,256]{1,0:T(2,128)S(1)}, f32[2,256]{1,0:T(2,128)S(1)}, u32[]{:S(2)}, u32[]{:S(2)}) collective-permute-start(f32[2,256]{1,0:T(2,128)S(1)} %get-tuple-element.5), channel_id=1, source_target_pairs={{0,8},{1,9},{2,10},{3,11},{4,12},{5,13},{6,14},{7,15},{8,0},{9,1},... | collective-permute-start | bytes 6152 | tf_op jit(solution)/shard_map/ppermute | solution.py:117
  305.5 5.2 %collective-permute-start.15 = (f32[2,256]{1,0:T(2,128)S(1)}, f32[2,256]{1,0:T(2,128)S(1)}, u32[]{:S(2)}, u32[]{:S(2)}) collective-permute-start(f32[2,256]{1,0:T(2,128)S(1)} %get-tuple-element.5), channel_id=1, source_target_pairs={{0,12},{1,13},{2,14},{3,15},{4,0},{5,1},{6,2},{7,3},{8,4},{9,5},{1... | collective-permute-start | bytes 6152 | tf_op jit(solution)/shard_map/ppermute | solution.py:117
  310.6 7.0 %collective-permute-start.16 = (f32[8,256]{1,0:T(8,128)S(1)}, f32[8,256]{1,0:T(8,128)S(1)}, u32[]{:S(2)}, u32[]{:S(2)}) collective-permute-start(f32[8,256]{1,0:T(8,128)S(1)} %constant_dynamic-update-slice_fusion.12), channel_id=1, source_target_pairs={{0,1},{1,2},{2,3},{3,0},{4,5},{5,6},{6,7},{7,4},{8,9},{9,10},{10,1... | collective-permute-start | bytes 24584 | tf_op jit(solution)/shard_map/ppermute | solution.py:117
  313.9 7.6 %collective-permute-start.17 = (f32[8,256]{1,0:T(8,128)S(1)}, f32[8,256]{1,0:T(8,128)S(1)}, u32[]{:S(2)}, u32[]{:S(2)}) collective-permute-start(f32[8,256]{1,0:T(8,128)S(1)} %constant_dynamic-update-slice_fusion.12), channel_id=1, source_target_pairs={{0,2},{1,3},{2,0},{3,1},{4,6},{5,7},{6,4},{7,5},{8,10},{9,11},{10,... | collective-permute-start | bytes 24584 | tf_op jit(solution)/shard_map/ppermute | solution.py:117
  315.8 5.7 %collective-permute-start.18 = (f32[8,256]{1,0:T(8,128)S(1)}, f32[8,256]{1,0:T(8,128)S(1)}, u32[]{:S(2)}, u32[]{:S(2)}) collective-permute-start(f32[8,256]{1,0:T(8,128)S(1)} %constant_dynamic-update-slice_fusion.12), channel_id=1, source_target_pairs={{0,3},{1,0},{2,1},{3,2},{4,7},{5,4},{6,5},{7,6},{8,11},{9,8},{10,9... | collective-permute-start | bytes 24584 | tf_op jit(solution)/shard_map/ppermute | solution.py:117
  321.5 5.2 %collective-permute-start.19 = (f32[32,256]{1,0:T(8,128)S(1)}, f32[32,256]{1,0:T(8,128)S(1)}, u32[]{:S(2)}, u32[]{:S(2)}) collective-permute-start(f32[32,256]{1,0:T(8,128)S(1)} %constant_dynamic-update-slice_fusion.8), channel_id=1, source_target_pairs={{0,64},{16,80},{32,96},{48,112},{64,128},{80,144},{96,160},{112,17... | collective-permute-start | bytes 98312 | tf_op jit(solution)/shard_map/ppermute | solution.py:117
  321.9 5.8 %collective-permute-start.20 = (f32[32,256]{1,0:T(8,128)S(1)}, f32[32,256]{1,0:T(8,128)S(1)}, u32[]{:S(2)}, u32[]{:S(2)}) collective-permute-start(f32[32,256]{1,0:T(8,128)S(1)} %constant_dynamic-update-slice_fusion.8), channel_id=1, source_target_pairs={{0,128},{16,144},{32,160},{48,176},{64,192},{80,208},{96,224},{112... | collective-permute-start | bytes 98312 | tf_op jit(solution)/shard_map/ppermute | solution.py:117
  329.4 7.3 %collective-permute-start.22 = (f32[128,256]{1,0:T(8,128)S(1)}, f32[128,256]{1,0:T(8,128)S(1)}, u32[]{:S(2)}, u32[]{:S(2)}) collective-permute-start(f32[128,256]{1,0:T(8,128)S(1)} %constant_dynamic-update-slice_fusion.4), channel_id=1, source_target_pairs={{0,32},{16,48},{32,0},{48,16},{64,96},{80,112},{96,64},{112,80},{1... | collective-permute-start | bytes 393224 | tf_op jit(solution)/shard_map/ppermute | solution.py:117
  336.7 5.7 %collective-permute-start.23 = (f32[256,256]{1,0:T(8,128)S(1)}, f32[256,256]{1,0:T(8,128)S(1)}, u32[]{:S(2)}, u32[]{:S(2)}) collective-permute-start(f32[256,256]{1,0:T(8,128)S(1)} %constant_dynamic-update-slice_fusion.2), channel_id=1, source_target_pairs={{0,16},{16,0},{32,48},{48,32},{64,80},{80,64},{96,112},{112,96},{1... | collective-permute-start | bytes 786440 | tf_op jit(solution)/shard_map/ppermute | solution.py:117
  336.8 23.4 %collective-permute-start.1 = (f32[256,256]{1,0:T(8,128)S(1)}, f32[256,256]{1,0:T(8,128)S(1)}, u32[]{:S(2)}, u32[]{:S(2)}) collective-permute-start(f32[256,256]{1,0:T(8,128)S(1)} %get-tuple-element.7), channel_id=1, source_target_pairs={{0,0},{1,16},{2,32},{3,48},{4,64},{5,80},{6,96},{7,112},{8,128},{9... | collective-permute-start | bytes 786440 | tf_op jit(solution)/shard_map/ppermute | solution.py:185
  (13 other events, 448.3 us)
Sparse Core Ops, SparseCore 0:
  9.8 42.3 all-gather.5
  75.2 100.9 reduce-scatter.2
  179.6 76.6 all-gather.3
  270.5 67.9 reduce-scatter.4
